TPU v7x, 128 devices: a whole 4x4x4 slice. The times are simulated.
128 devices in a mesh: feat: 4 (over x), dp: 32 (over z, y, core).
Axes of the slice: x: 4, y: 4, z: 4, core: 2. Of those that a mesh axis runs over, the one named last changes fastest.
Arguments:
- gradients: bfloat16 [64, 16777216], P('dp', 'feat'), may hold values from -6 to 6
- sign_seed: int32 [3], replicated, may hold values from 0 to 1073741823
- sample_index: int32 [8192], replicated, may hold values from 0 to 16777215
- target_sketches: bfloat16 [512, 8192], P('dp'), may hold values from -50 to 50
- target_group: int32 [512], replicated, may hold values from 0 to 15, never falling along the last dimension, each value on 1 to 128 neighbouring positions
Outputs:
- scores: float32 [64, 512], P('dp')
- group_scores: float32 [64, 16], P('dp')
Inputs may be any that keep to these rules, and one draw needn't show every extreme that they name: target_group never falls along the targets; each of the 16 groups has 1 to 128 targets, one exactly 128.
All inputs are finite; a program needn't handle non-finite values.
Results may differ from a plain program's by a relative error of at most 0.022.
Values may be sent and summed in bfloat16 or wider, within the bound.
A program may use at most 128 MiB of HBM per device.

v0:
```python
import math

import jax
import jax.numpy as jnp
from jax import lax
from jax.sharding import PartitionSpec as P

P_SIZE = 16777216
TASKS = 16


EPS = 1e-06


def flip_bits(index, seeds):
    value = index * 747796405 + seeds[0]
    value = value ^ value >> 15 & 131071
    value = value * 277803737 + seeds[1]
    value = value ^ value >> 13 & 524287
    value = value * 1103515245 + seeds[2]
    return value >> 20 & 1


def parity_bits(left, right, count):
    total = jnp.zeros_like(left)
    for place in range(count):
        total = total + (left >> place & 1) * (right >> place & 1)
    return total & 1


def hadamard(order):
    rows = lax.broadcasted_iota(jnp.int32, (order, order), 0)
    cols = lax.broadcasted_iota(jnp.int32, (order, order), 1)
    parity = parity_bits(rows, cols, max(order.bit_length() - 1, 0))
    return (1 - 2 * parity).astype(jnp.bfloat16)


def finish(dots, squares, target_squares, width):
    return (
        dots
        * lax.rsqrt(squares[:, None] + EPS)
        * lax.rsqrt(target_squares[None, :] + EPS)
        * math.sqrt(width)
    )


def row_squares(matrix):
    wide = matrix.astype(jnp.float32)
    return jnp.sum(wide * wide, axis=1)


def shards(gradients, sign_seed, sample_index, target_sketches, target_group):
    ex_rows, local = gradients.shape
    width = sample_index.shape[0]
    feat_rank = lax.axis_index("feat")
    feat_bits = lax.axis_size("feat").bit_length() - 1
    index = feat_rank * local + lax.iota(jnp.int32, local)
    bits = flip_bits(index, sign_seed)
    signed = jnp.where(bits[None, :] == 1, -gradients, gradients)
    outer = local // 16384
    block = signed.reshape(ex_rows, outer, 128, 128)
    h_small = hadamard(128)
    h_outer = hadamard(outer)
    first = jnp.einsum("eabc,dc->eabd", block, h_small, preferred_element_type=jnp.float32).astype(
        jnp.bfloat16
    )
    second = jnp.einsum("db,eabc->deac", h_small, first, preferred_element_type=jnp.float32).astype(
        jnp.bfloat16
    )
    high = sample_index // local
    low = sample_index % local
    outer_pos = low // 16384
    row_pos = low % 16384 // 128
    col_pos = low % 128
    columns = second[row_pos, :, :, col_pos]
    outer_rows = jnp.take(h_outer, outer_pos, axis=0)
    third = jnp.einsum(
        "kea,ka->ek", columns, outer_rows, preferred_element_type=jnp.float32
    ).astype(jnp.bfloat16)
    weight = (1 - 2 * parity_bits(high, feat_rank + 0 * high, feat_bits)).astype(jnp.float32)
    term = third.astype(jnp.float32) * (weight * (1.0 / math.sqrt(P_SIZE)))[None, :]
    sketch = lax.psum(term.astype(jnp.bfloat16), "feat")
    squares = row_squares(sketch)
    piece = lax.all_gather(target_sketches, "dp", axis=0, tiled=True)
    dots = jnp.einsum("ek,tk->et", sketch, piece, preferred_element_type=jnp.float32)
    scores = finish(dots, squares, row_squares(piece), width)
    onehot = (target_group[:, None] == lax.broadcasted_iota(jnp.int32, (1, TASKS), 1)).astype(
        jnp.float32
    )
    counts = jnp.sum(onehot, axis=0)
    group_scores = jnp.dot(scores, onehot, precision=lax.Precision.HIGHEST) / counts[None, :]
    return (scores, group_scores)


def solution(mesh):
    in_specs = (P("dp", "feat"), P(), P(), P("dp", None), P())
    out_specs = (P("dp", None), P("dp", None))
    return jax.shard_map(shards, mesh=mesh, in_specs=in_specs, out_specs=out_specs, check_vma=False)
```

profile of v0, /device:TPU:1, one launch (start us, length us, event | category | flops | bytes accessed | tf_op | source)
XLA Modules:
  0.0 311.5 jit_solution(16227121051779870722)
XLA Ops:
  7.2 0.0 all-gather.2.cloned.1.call-start
  7.2 0.7 all-gather.2.cloned.1.call-update
  7.9 1.4 fusion.79
  9.3 11.8 %and_compare_fusion = pred[4194304]{0:T(1024)(128)(4,1)S(1)} fusion(s32[]{:T(128)} %bitcast.5, s32[]{:T(128)} %bitcast.4, s32[]{:T(128)} %bitcast.3, s32[]{:T(128)S(6)} %mul.172), kind=kLoop, calls=%fused_computation.8 | loop fusion | flops 67108864 | bytes 4194320 | tf_op jit(solution)/shard_map/eq | solution.py:59
  21.1 32.9 %fusion = bf16[1,2,32768,128]{3,1,2,0:T(2,128)(2,1)} fusion(bf16[2,4194304]{1,0:T(2,128)(2,1)} %param.5, pred[4194304]{0:T(1024)(128)(4,1)S(1)} %and_compare_fusion), kind=kLoop, calls=%fused_computation.3 | loop fusion | flops 16777216 | bytes 37748736
  54.0 15.3 %copy.11 = bf16[1,2,32768,128]{3,2,1,0:T(8,128)(2,1)} copy(bf16[1,2,32768,128]{3,1,2,0:T(2,128)(2,1)} %fusion) | data formatting | bytes 33554432
  69.3 16.9 %fusion.5 = bf16[128,2,256,128]{3,0,2,1:T(8,128)(2,1)} fusion(bf16[2,256,128,128]{3,2,1,0:T(8,128)(2,1)} %bitcast.26, s32[128]{0:T(128)S(1)} %fusion.74, s32[128]{0:T(128)S(1)} %get-tuple-element.12, s32[128]{0:T(128)S(1)} %get-tuple-element.11, s32[128]{0:T(128)S(1)} %get-tuple-element.10, s32[128]{0:T(128)S(1)} %get-tuple-element.9, ...), kind=kOutput, calls=%fused_computation.9 | convolution fusion | flops 4312301568 | bytes 33558016 | tf_op jit(solution)/shard_map/db,eabc->deac/dot_general | solution.py:67
  86.3 0.0 copy-start
  86.3 30.1 %copy.7 = bf16[128,2,256,128]{2,1,3,0:T(2,128)(2,1)} copy(bf16[128,2,256,128]{3,0,2,1:T(8,128)(2,1)} %fusion.5) | data formatting | bytes 33554432 | tf_op jit(solution)/shard_map/convert_element_type | solution.py:67
  116.3 0.0 copy-done
  116.3 0.1 fusion.19
  116.4 79.3 %gather_fusion.1 = bf16[8192,2,256]{2,1,0:T(2,128)(2,1)} fusion(bf16[128,2,256,128]{2,1,3,0:T(2,128)(2,1)} %copy.7, s32[8192]{0:T(1024)S(1)} %fusion.19), kind=kCustom, calls=%fused_computation.1 | custom fusion | bytes 16842752 | tf_op jit(solution)/shard_map/gather | solution.py:75
  195.8 0.3 subtract_convert_fusion
  196.1 32.9 %gather_fusion = bf16[8192,256]{1,0:T(8,128)(2,1)} fusion(bf16[256,256]{1,0:T(8,128)(2,1)S(1)} %subtract_convert_fusion, s32[8192]{0:T(1024)S(1)} %broadcast_clamp_fusion), kind=kCustom, calls=%fused_computation | custom fusion | bytes 8421376 | tf_op jit(solution)/shard_map/jit(_take)/gather | solution.py:76
  229.0 6.0 %select_bitcast_fusion = bf16[8192,256,1]{1,0,2:T(8,128)(2,1)S(1)} fusion(bf16[8192,256]{1,0:T(8,128)(2,1)} %gather_fusion, pred[8192]{0:T(1024)(128)(4,1)S(1)} %get-tuple-element.2), kind=kLoop, calls=%fused_computation.12 | loop fusion | flops 2097152 | bytes 8396800 | tf_op jit(solution)/shard_map/jit(_take)/select_n | solution.py:76
  235.0 0.0 copy-start.2
  235.0 35.5 %fusion.8 = bf16[8192,1,2]{2,1,0:T(2,128)(2,1)} fusion(bf16[8192,2,256]{2,1,0:T(2,128)(2,1)} %gather_fusion.1, bf16[8192,256,1]{1,0,2:T(8,128)(2,1)S(1)} %select_bitcast_fusion), kind=kOutput, calls=%fused_computation.10 | convolution fusion | flops 8388608 | bytes 12615680 | tf_op jit(solution)/shard_map/kea,ka->ek/dot_general | solution.py:77
  270.5 8.1 %copy.10 = bf16[8192,1,2]{0,2,1:T(2,128)(2,1)S(1)} copy(bf16[8192,1,2]{2,1,0:T(2,128)(2,1)} %fusion.8) | data formatting | bytes 65536 | tf_op jit(solution)/shard_map/kea,ka->ek/dot_general | solution.py:77
  278.7 14.1 %psum.7 = bf16[2,8192]{1,0:T(2,128)(2,1)S(1)} all-reduce(bf16[2,8192]{1,0:T(2,128)(2,1)S(1)} %fusion.16), channel_id=1, replica_groups=mesh['feat'=4,'dp'=32] {'feat'}, use_global_device_ids=true, to_apply=%region_0.1 | all-reduce | flops 16384 | bytes 65536 | tf_op jit(solution)/shard_map/psum | solution.py:82
  292.8 0.0 copy-done.2
  292.8 0.1 convert_reduce_fusion
  293.0 0.2 multiply_reduce_fusion.1
  293.2 0.0 all-gather.2.cloned.1.call-done
  293.2 5.1 %multiply_reduce_fusion = f32[512]{0:T(512)S(1)} fusion(bf16[512,8192]{1,0:T(8,128)(2,1)} %all-gather.2.cloned.1.call-done), kind=kLoop, calls=%fused_computation.4 | loop fusion | flops 12582400 | bytes 8390656 | tf_op jit(solution)/shard_map/reduce_sum | solution.py:49
  298.3 5.6 %fusion.11 = f32[2,512]{1,0:T(2,128)S(1)} fusion(bf16[2,8192]{1,0:T(2,128)(2,1)S(1)} %psum.7, bf16[512,8192]{1,0:T(8,128)(2,1)} %all-gather.2.cloned.1.call-done, f32[2]{0:T(128)S(1)} %add_rsqrt_fusion.1, f32[512]{0:T(512)S(1)} %add_rsqrt_fusion), kind=kOutput, calls=%fused_computation.15 | convolution fusion | flops 16780288 | bytes 8427528 | tf_op jit(solution)/shard_map/ek,tk->et/dot_general | solution.py:85
  303.9 0.0 copy-start.1
  303.9 0.7 convolution_divide_fusion
  304.7 0.0 copy-done.1
  (14 shorter events, 0.2 us)
Async XLA Ops:
  7.2 286.0 %all-gather.2.cloned.1.call-start = ((), (), s32[]{:S(2)}) async-start(), calls=%async_computation | async-start | bytes 8650752 | tf_op jit(solution)/shard_map/all_gather | solution.py:84
  86.3 30.1 %copy-start = (s32[8192]{0:T(1024)S(1)}, s32[8192]{0:T(1024)}, u32[]{:S(2)}) copy-start(s32[8192]{0:T(1024)} %param.7) | copy-start | bytes 98308
  235.0 57.9 %copy-start.2 = (s32[512]{0:T(512)S(1)}, s32[512]{0:T(512)}, u32[]{:S(2)}) copy-start(s32[512]{0:T(512)} %param.9) | copy-start | bytes 6148
  303.9 0.7 copy-start.1
Sparse Core Ops, SparseCore 0:
  10.3 56.6 all-gather.1
where the time goes:
time: 316 us; the launch traced here: 312 us
  local copies, waits for them, and re-layouts  167 us (53%)
  matrix products  58.9 us (19%)
  other arithmetic  56.6 us (18%)
  blocking collectives  14.1 us (4%)
  between operations  14.1 us (4%)
    gather x1, local copies, waits for them, and re-layouts, shards(): columns = second[row_pos, :, :, col_pos]  79.3 us
    dot_general x1, matrix products, shards(): jnp.einsum('kea,ka->ek', columns, outer_rows, preferred_element_type=jnp....  35.5 us
    unnamed x1, other arithmetic  32.9 us
    gather x1, local copies, waits for them, and re-layouts, shards(): outer_rows = jnp.take(h_outer, outer_pos, axis=0)  32.9 us
    convert_element_type x1, local copies, waits for them, and re-layouts, shards(): jnp.einsum('db,eabc->deac', h_small, first, preferred_element_type=jnp.fl...  30.1 us
    dot_general x1, matrix products, shards(): jnp.einsum('db,eabc->deac', h_small, first, preferred_element_type=jnp.fl...  16.9 us
    unnamed x7, local copies, waits for them, and re-layouts  15.3 us
    psum x1, blocking collectives, shards(): sketch = lax.psum(term.astype(jnp.bfloat16), 'feat')  14.1 us
  transfers between devices with their start and end apart: 1, of which 0 were waited for; matrix products, arithmetic and copies ran while one was open for 87% of the time, Pallas kernels for 0%

commit v1 on v0

v1 whole, which is shorter than its diff:
```python
import functools
import math

import jax
import jax.numpy as jnp
from jax import lax
from jax.experimental import pallas as pl
from jax.experimental.pallas import tpu as pltpu
from jax.sharding import PartitionSpec as P

EPS = 1e-06
TASKS = 16
MULS = (747796405, 277803737, 1103515245)
CHUNKS = 16
UNROLL = 4


def wrap(value):
    value &= 0xFFFFFFFF
    return value - (1 << 32) if value >= 1 << 31 else value


def butterflies(vals):
    vals = list(vals)
    half = 1
    while half < len(vals):
        for start in range(0, len(vals), 2 * half):
            for j in range(start, start + half):
                a, b = vals[j], vals[j + half]
                vals[j], vals[j + half] = a + b, a - b
        half *= 2
    return vals


def parity_signs(left, right):
    x = left & right
    x = x ^ (x >> 4)
    x = x ^ (x >> 2)
    x = x ^ (x >> 1)
    return jnp.where((x & 1) == 1, -1.0, 1.0).astype(jnp.float32)


def aligned(value, by):
    return pl.multiple_of(value, by)


def local_kernel(seed_ref, lane_ref, x_hbm, o_ref, xa, xb, sa, sb, y, t, g, h_ref, w_ref, code, idx_v, idx_s, sems, isem):
    feat = lax.axis_index("feat")
    low = lane_ref[...] & 4194303
    idx_v[...] = ((low >> 13) << 7) | (low & 127)
    index_copy = pltpu.make_async_copy(idx_v, idx_s, isem)
    index_copy.start()

    def fetch(n, buf, which):
        return pltpu.make_async_copy(x_hbm.at[pl.ds(n * 32, 32), :, :], buf, sems.at[which])

    fetch(0, xa, 0).start()
    fetch(1, xb, 1).start()
    r = lax.broadcasted_iota(jnp.int32, (256, 256), 0)
    c = lax.broadcasted_iota(jnp.int32, (256, 256), 1)
    h_ref[...] = parity_signs(r, c).astype(jnp.bfloat16)
    r = lax.broadcasted_iota(jnp.int32, (128, 128), 0)
    c = lax.broadcasted_iota(jnp.int32, (128, 128), 1)
    w_ref[...] = jnp.where((r >> 6) == (c & 1), parity_signs(r & 63, c >> 1), 0.0).astype(jnp.bfloat16)
    s0, s1, s2 = seed_ref[0], seed_ref[1], seed_ref[2] * 2048
    rows = lax.broadcasted_iota(jnp.int32, (8, 128), 0)
    cols = lax.broadcasted_iota(jnp.int32, (8, 128), 1)
    base = (rows * 128 + cols + feat * 4194304) * MULS[0] + s0
    upper = lax.shift_right_logical(rows, 1)
    lower = upper + 4

    def sign(n, qg, x_ref, s_ref):
        start = base + (n * 262144 + qg * 1024) * MULS[0]
        for u in range(2):
            vals = []
            for w4 in range(16):
                w = w4 * 2 + u
                v = start + wrap(w * 8192 * MULS[0])
                v = v ^ lax.shift_right_logical(v, 15)
                v = v * MULS[1] + s1
                v = v ^ lax.shift_right_logical(v, 13)
                v = v * wrap(MULS[2] * 2048) + s2
                flips = jnp.where(v < 0, -1.0, 1.0).astype(jnp.float32)
                pairs = [jnp.take_along_axis(flips, at, axis=0) for at in (upper, lower)]
                both = jnp.concatenate(pairs, axis=0).astype(jnp.bfloat16)
                vals.append(x_ref[w, pl.ds(aligned(qg * 16, 16), 16), :] * both)
            vals = butterflies(vals)
            for w4 in range(16):
                s_ref[w4, pl.ds(aligned(qg * 16, 16), 16), u * 128 : (u + 1) * 128] = vals[w4]

    def transform(n, pair, s_ref):
        rhs = s_ref[pl.ds(pair * 2, 2), :, :].reshape(256, 256)
        out = lax.dot_general(
            h_ref[...], rhs, (((1,), (1,)), ((), ())), preferred_element_type=jnp.float32
        ).astype(jnp.bfloat16)
        y[n, pair * 2] = out[:, :128]
        y[n, pair * 2 + 1] = out[:, 128:]

    def stage(n, x_ref, s_write, s_read):
        def body(i, carry):
            if s_read is not None:
                for a in range(UNROLL):
                    transform(n - 1, i * UNROLL + a, s_read)
            if x_ref is not None:
                for a in range(UNROLL):
                    sign(n, i * UNROLL + a, x_ref, s_write)
            return carry

        lax.fori_loop(0, 8 // UNROLL, body, 0)

    fetch(0, xa, 0).wait()
    stage(0, xa, sa, None)
    fetch(2, xa, 0).start()

    def outer(j, carry):
        n = 2 * j + 1
        fetch(n, xb, 1).wait()
        stage(n, xb, sb, sa)
        fetch(n + 2, xb, 1).start()
        fetch(n + 1, xa, 0).wait()
        stage(n + 1, xa, sa, sb)

        @pl.when(j < CHUNKS // 2 - 2)
        def _():
            fetch(n + 3, xa, 0).start()

        return carry

    lax.fori_loop(0, CHUNKS // 2 - 1, outer, 0)
    fetch(CHUNKS - 1, xb, 1).wait()
    stage(CHUNKS - 1, xb, sb, sa)
    stage(CHUNKS, None, None, sb)

    def across(i, carry):
        m = i >> 2
        o = aligned((i & 3) * 64, 64)
        for a in range(4):
            vals = butterflies([y[n, m, pl.ds(o + a * 16, 16), :] for n in range(CHUNKS)])
            for n in range(CHUNKS):
                t[n, pl.ds(aligned(i * 64 + a * 16, 16), 16), :] = vals[n].astype(jnp.float32)
        return carry

    lax.fori_loop(0, 64, across, 0)
    flat = t.reshape(65536, 128)
    index_copy.wait()

    def pick(kb, carry):
        def row(j, inner):
            for a in range(128):
                at = idx_s[kb * 8 + j, a]
                g[pl.ds(j * 128 + a, 1), :] = flat[pl.ds(at, 1), :]
            return inner

        lax.fori_loop(0, 8, row, 0)
        out = lax.dot_general(
            w_ref[...],
            g[...].astype(jnp.bfloat16),
            (((1,), (1,)), ((), ())),
            preferred_element_type=jnp.float32,
        )
        place = lax.broadcasted_iota(jnp.int32, (64, 128), 0)
        for j in range(8):
            picked = lane_ref[pl.ds(kb * 8 + j, 1), :]
            hit = place == ((picked >> 7) & 63)
            common = (picked >> 22) & feat
            scale = jnp.where((((common >> 1) ^ common) & 1) == 1, -1.0 / 4096, 1.0 / 4096)
            for e in range(2):
                third = jnp.sum(
                    jnp.where(hit, out[e * 64 : (e + 1) * 64, j * 128 : (j + 1) * 128], 0.0),
                    axis=0,
                    keepdims=True,
                )
                code[kb >> 1, e, pl.ds((kb & 1) * 8 + j, 1), :] = third * scale
        return carry

    lax.fori_loop(0, 8, pick, 0)
    o_ref[...] = code[...].astype(jnp.bfloat16)


def local_terms(gradients, sign_seed, sample_index):
    x = gradients.reshape(2, 32768, 128).transpose(1, 0, 2).reshape(512, 128, 128)
    vmem = pltpu.VMEM
    return pl.pallas_call(
        local_kernel,
        out_shape=jax.ShapeDtypeStruct((4, 2, 16, 128), jnp.bfloat16),
        in_specs=[
            pl.BlockSpec(memory_space=pltpu.SMEM),
            pl.BlockSpec(memory_space=pltpu.VMEM),
            pl.BlockSpec(memory_space=pl.ANY),
        ],
        out_specs=pl.BlockSpec(memory_space=pltpu.VMEM),
        scratch_shapes=[
            vmem((32, 128, 128), jnp.bfloat16),
            vmem((32, 128, 128), jnp.bfloat16),
            vmem((16, 128, 256), jnp.bfloat16),
            vmem((16, 128, 256), jnp.bfloat16),
            vmem((16, 16, 256, 128), jnp.bfloat16),
            vmem((16, 4096, 128), jnp.float32),
            vmem((1024, 128), jnp.float32),
            vmem((256, 256), jnp.bfloat16),
            vmem((128, 128), jnp.bfloat16),
            vmem((4, 2, 16, 128), jnp.float32),
            vmem((64, 128), jnp.int32),
            pltpu.SMEM((64, 128), jnp.int32),
            pltpu.SemaphoreType.DMA((2,)),
            pltpu.SemaphoreType.DMA,
        ],
        compiler_params=pltpu.CompilerParams(vmem_limit_bytes=61 * 1024 * 1024),
        cost_estimate=pl.CostEstimate(flops=9_000_000_000, bytes_accessed=17_000_000, transcendentals=0),
    )(sign_seed, sample_index.reshape(64, 128), x)


NT_DIMS = (((1,), (1,)), ((), ()))


def score_kernel(term_ref, group_ref, target_hbm, scores_ref, means_ref, tgt, got, lhs, part, sems, tsem):
    feat = lax.axis_index("feat")
    target_copy = pltpu.make_async_copy(target_hbm, tgt, tsem)
    target_copy.start()
    barrier = pltpu.get_barrier_semaphore()
    peers = [lax.rem(feat + d, 4) for d in (1, 2, 3)]
    for peer in peers:
        pl.semaphore_signal(barrier, inc=1, device_id={"feat": peer}, device_id_type=pl.DeviceIdType.MESH)
    pl.semaphore_wait(barrier, 3)

    def to_peer(source, landing, slot, d):
        return pltpu.make_async_remote_copy(
            src_ref=source,
            dst_ref=landing,
            send_sem=sems.at[slot, 0, d],
            recv_sem=sems.at[slot, 1, d],
            device_id={"feat": peers[d]},
            device_id_type=pl.DeviceIdType.MESH,
        )

    terms = [to_peer(term_ref.at[peers[d]], got.at[d], 0, d) for d in range(3)]
    for copy in terms:
        copy.start()
    target_copy.wait()
    squares = []
    for b in range(4):
        total = jnp.zeros((128, 128), jnp.float32)
        for r in range(16):
            wide = tgt[b * 128 : (b + 1) * 128, r * 128 : (r + 1) * 128].astype(jnp.float32)
            total = total + wide * wide
        squares.append(total)
    squares = jnp.concatenate(squares, axis=0)
    ones = jnp.ones((8, 128), jnp.float32)
    target_squares = lax.dot_general(
        ones, squares, NT_DIMS, precision=lax.Precision.HIGHEST, preferred_element_type=jnp.float32
    )
    for copy in terms:
        copy.wait()
    own = term_ref[feat].astype(jnp.float32)
    for d in range(3):
        own = own + got[d].astype(jnp.float32)
    sketch = own.astype(jnp.bfloat16).astype(jnp.float32)
    lhs[...] = jnp.zeros_like(lhs)
    for e in range(2):
        for r in range(16):
            lhs[e : e + 1, r * 128 : (r + 1) * 128] = sketch[e, r : r + 1, :]
    wide = lhs[...]
    own_squares = jnp.sum(wide * wide, axis=1, keepdims=True)
    dots = lax.dot_general(
        wide.astype(jnp.bfloat16), tgt[...], NT_DIMS, preferred_element_type=jnp.float32
    )
    part[feat, 0] = dots
    part[feat, 1] = target_squares
    part[feat, 2] = jnp.broadcast_to(own_squares, (8, 512))
    parts = [to_peer(part.at[feat], part.at[feat], 1, d) for d in range(3)]
    for copy in parts:
        copy.start()
    member = (lax.broadcasted_iota(jnp.int32, (128, 512), 0) == group_ref[...]).astype(jnp.float32)
    for copy in parts:
        copy.wait()
    whole = (part[0] + part[1]) + (part[2] + part[3])
    scores = whole[0] * lax.rsqrt(whole[2] + EPS) * lax.rsqrt(whole[1] + EPS) * math.sqrt(8192)
    at = lax.broadcasted_iota(jnp.int32, (8, 512), 0)
    sums = lax.dot_general(
        jnp.where(at < 2, scores, 1.0),
        member,
        NT_DIMS,
        precision=lax.Precision.HIGHEST,
        preferred_element_type=jnp.float32,
    )
    scores_ref[...] = scores[:2]
    means_ref[...] = sums[:2, :TASKS] / sums[2:3, :TASKS]


def shards(gradients, sign_seed, sample_index, target_sketches, target_group):
    feat = lax.axis_index("feat")
    share = lax.dynamic_slice(target_sketches, (0, feat * 2048), (16, 2048))
    targets = lax.all_gather(share, "dp", axis=0, tiled=True)
    terms = local_terms(gradients, sign_seed, sample_index)
    vmem = pltpu.VMEM
    return pl.pallas_call(
        score_kernel,
        out_shape=(
            jax.ShapeDtypeStruct((2, 512), jnp.float32),
            jax.ShapeDtypeStruct((2, TASKS), jnp.float32),
        ),
        in_specs=[
            pl.BlockSpec(memory_space=pltpu.VMEM),
            pl.BlockSpec(memory_space=pltpu.VMEM),
            pl.BlockSpec(memory_space=pl.ANY),
        ],
        out_specs=(pl.BlockSpec(memory_space=pltpu.VMEM), pl.BlockSpec(memory_space=pltpu.VMEM)),
        scratch_shapes=[
            vmem((512, 2048), jnp.bfloat16),
            vmem((3, 2, 16, 128), jnp.bfloat16),
            vmem((8, 2048), jnp.float32),
            vmem((4, 3, 8, 512), jnp.float32),
            pltpu.SemaphoreType.DMA((2, 2, 3)),
            pltpu.SemaphoreType.DMA,
        ],
        compiler_params=pltpu.CompilerParams(
            collective_id=0, has_side_effects=True, vmem_limit_bytes=32 * 1024 * 1024
        ),
    )(terms, target_group.reshape(1, 512), targets)


def solution(mesh):
    in_specs = (P("dp", "feat"), P(), P(), P("dp", None), P())
    out_specs = (P("dp", None), P("dp", None))
    return jax.shard_map(shards, mesh=mesh, in_specs=in_specs, out_specs=out_specs, check_vma=False)
```

time: 316 us -> 80.3 us (0.25)
  local copies, waits for them, and re-layouts: 167 us -> 5.02 us
  matrix products: 58.9 us -> 0 us
  other arithmetic: 56.6 us -> 0 us
  Pallas kernels: 0 us -> 46.9 us
  blocking collectives: 14.1 us -> 0 us
  waiting for transfers between devices: 0.7 us -> 12.8 us
    gather x2 -> x0, local copies, waits for them, and re-layouts: 112 us -> none  [the longest x1 79.3 us: shards(): columns = second[row_pos, :, :, col_pos]]
    dot_general x4 -> x0, matrix products: 58.9 us -> none  [the longest x1 35.5 us: shards(): jnp.einsum('kea,ka->ek', columns, outer_rows, preferred_element_type=jnp....]
    pallas_call x0 -> x2, Pallas kernels: none -> 46.9 us  [the longest x1 36.4 us: local_terms(): pl.pallas_call(local_kernel, out_shape=jax.ShapeDtypeStruct((4, 2, 16, 12...]
    unnamed x1 -> x0, other arithmetic: 32.9 us -> none
    convert_element_type x1 -> x0, local copies, waits for them, and re-layouts: 30.1 us -> none  [shards(): jnp.einsum('db,eabc->deac', h_small, first, preferred_element_type=jnp.fl...]
    psum x1 -> x0, blocking collectives: 14.1 us -> none  [shards(): sketch = lax.psum(term.astype(jnp.bfloat16), 'feat')]
    all_gather x1, waiting for transfers between devices: 0.02 us -> 12.8 us  [shards(): targets = lax.all_gather(share, 'dp', axis=0, tiled=True)]
    eq x1 -> x0, other arithmetic: 11.8 us -> none  [shards(): signed = jnp.where(bits[None, :] == 1, -gradients, gradients)]
  transfers between devices with their start and end apart: 1 -> 1, of which waited for: 0 -> 1; matrix products, arithmetic and copies ran while one was open for 87% -> 0% of each run, Pallas kernels for 0% -> 46%
where the time goes in v1:
time: 80.3 us; the launch traced here: 78.8 us
  Pallas kernels  46.9 us (58%)
  between operations  14.1 us (18%)
  waiting for transfers between devices  12.8 us (16%)
  local copies, waits for them, and re-layouts  5.02 us (6%)
    pallas_call x1, Pallas kernels, local_terms(): pl.pallas_call(local_kernel, out_shape=jax.ShapeDtypeStruct((4, 2, 16, 12...  36.4 us
    all_gather x1, waiting for transfers between devices, shards(): targets = lax.all_gather(share, 'dp', axis=0, tiled=True)  12.8 us
    pallas_call x1, Pallas kernels, shards(): pl.pallas_call(score_kernel, out_shape=(jax.ShapeDtypeStruct((2, 512), jn...  10.5 us
    unnamed x10, local copies, waits for them, and re-layouts  4.4 us
  transfers between devices with their start and end apart: 1, of which 1 were waited for; matrix products, arithmetic and copies ran while one was open for 0% of the time, Pallas kernels for 46%

profile of v1, /device:TPU:1, one launch (start us, length us, event | category | flops | bytes accessed | tf_op | source)
XLA Modules:
  0.0 78.8 jit_solution(2607785376136262832)
XLA Ops:
  7.2 0.0 copy-start
  7.2 0.0 copy-start.3
  7.2 0.0 all-gather.2.cloned.1.call-start
  7.2 0.9 %copy-done = bf16[16,8192]{1,0:T(8,128)(2,1)S(1)} copy-done((bf16[16,8192]{1,0:T(8,128)(2,1)S(1)}, bf16[16,8192]{1,0:T(8,128)(2,1)}, u32[]{:S(2)}) %copy-start) | copy-done | bytes 262168
  8.1 0.6 constant_dynamic-slice_fusion
  8.7 0.0 all-gather.2.cloned.1.call-update
  8.8 36.4 %shard_map.68.term_ref = bf16[4,2,16,128]{3,2,1,0:T(8,128)(2,1)} custom-call(s32[3]{0:T(128)} %seed_ref.1, s32[64,128]{1,0:T(8,128)} %bitcast.9, bf16[512,128,128]{2,1,0:T(8,128)(2,1)} %bitcast.8), custom_call_target="tpu_custom_call" | custom-call | flops 8999999488 | bytes 17000000 | tf_op jit(solution)/shard_map/pallas_call | solution.py:183
  45.2 12.8 %all-gather.2.cloned.1.call-done.target_hbm = bf16[512,2048]{1,0:T(8,128)(2,1)} async-done(((bf16[16,2048]{1,0:T(8,128)(2,1)}), bf16[512,2048]{1,0:T(8,128)(2,1)}) %all-gather.2.cloned.1.call-update) | async-done | bytes 2097168 | tf_op jit(solution)/shard_map/all_gather | solution.py:293
  58.0 0.0 copy-done.3
  58.0 0.0 copy-start.1
  58.0 1.6 %copy-done.1 = bf16[512,2048]{1,0:T(8,128)(2,1)S(1)} copy-done((bf16[512,2048]{1,0:T(8,128)(2,1)S(1)}, bf16[512,2048]{1,0:T(8,128)(2,1)}, u32[]{:S(2)}) %copy-start.1) | copy-done | bytes 2097176
  59.6 0.0 copy-start.2
  59.6 0.8 copy-done.2
  60.3 10.5 %shard_map.69 = (f32[2,512]{1,0:T(2,128)S(1)}, f32[2,16]{1,0:T(2,128)S(1)}) custom-call(bf16[4,2,16,128]{3,2,1,0:T(8,128)(2,1)S(1)} %copy-done.2, s32[1,512]{1,0:T(1,128)S(1)} %bitcast.7, bf16[512,2048]{1,0:T(8,128)(2,1)S(1)} %copy-done.1), custom_call_target="tpu_custom_call" | custom-call | tf_op jit(solution)/shard_map/pallas_call | solution.py:296
  70.8 0.6 copy.10
  71.4 0.6 copy.11
Async XLA Ops:
  7.2 1.0 %copy-start = (bf16[16,8192]{1,0:T(8,128)(2,1)S(1)}, bf16[16,8192]{1,0:T(8,128)(2,1)}, u32[]{:S(2)}) copy-start(bf16[16,8192]{1,0:T(8,128)(2,1)} %param.8) | copy-start | bytes 786436
  7.2 50.8 %copy-start.3 = (s32[512]{0:T(512)S(1)}, s32[512]{0:T(512)}, u32[]{:S(2)}) copy-start(s32[512]{0:T(512)} %param.9) | copy-start | bytes 6148
  7.2 50.8 %all-gather.2.cloned.1.call-start = ((), (), s32[]{:S(2)}) async-start(), calls=%async_computation | async-start | bytes 2162688 | tf_op jit(solution)/shard_map/all_gather | solution.py:293
  58.0 1.6 %copy-start.1 = (bf16[512,2048]{1,0:T(8,128)(2,1)S(1)}, bf16[512,2048]{1,0:T(8,128)(2,1)}, u32[]{:S(2)}) copy-start(bf16[512,2048]{1,0:T(8,128)(2,1)} %all-gather.2.cloned.1.call-done.target_hbm) | copy-start | bytes 6291460
  59.6 0.8 copy-start.2
Sparse Core Ops, SparseCore 0:
  10.3 47.6 all-gather.1

commit v2 on v1

--- a/solution.py
+++ b/solution.py
@@ -9,6 +9,8 @@
 from jax.sharding import PartitionSpec as P
 
 EPS = 1e-06
+NT_DIMS = (((1,), (1,)), ((), ()))
+MESH = pl.DeviceIdType.MESH
 TASKS = 16
 MULS = (747796405, 277803737, 1103515245)
 CHUNKS = 16
@@ -44,8 +46,11 @@
     return pl.multiple_of(value, by)
 
 
-def local_kernel(seed_ref, lane_ref, x_hbm, o_ref, xa, xb, sa, sb, y, t, g, h_ref, w_ref, code, idx_v, idx_s, sems, isem):
+def whole_kernel(seed_ref, lane_ref, group_ref, target_hbm, x_hbm, scores_ref, means_ref, xa, xb, sa, sb, y, t, g,
+                 h_ref, w_ref, code, idx_v, idx_s, term, got, lhs, tgt, part,
+                 sems, isem, tsem, send_sems, recv_sems, feat_sems):
     feat = lax.axis_index("feat")
+    me = lax.axis_index("dp")
     low = lane_ref[...] & 4194303
     idx_v[...] = ((low >> 13) << 7) | (low & 127)
     index_copy = pltpu.make_async_copy(idx_v, idx_s, isem)
@@ -56,6 +61,19 @@
 
     fetch(0, xa, 0).start()
     fetch(1, xb, 1).start()
+    share = target_hbm.at[:, pl.ds(aligned(feat * 2048, 2048), 2048)]
+    own_targets = pltpu.make_async_copy(share, tgt.at[me], tsem)
+    own_targets.start()
+    barrier = pltpu.get_barrier_semaphore()
+    peers = [lax.rem(feat + d, 4) for d in (1, 2, 3)]
+    for peer in peers:
+        pl.semaphore_signal(barrier, inc=1, device_id={"feat": peer}, device_id_type=MESH)
+
+    def greet(j, carry):
+        pl.semaphore_signal(barrier, inc=1, device_id={"dp": lax.rem(me + j, 32)}, device_id_type=MESH)
+        return carry
+
+    lax.fori_loop(1, 32, greet, 0)
     r = lax.broadcasted_iota(jnp.int32, (256, 256), 0)
     c = lax.broadcasted_iota(jnp.int32, (256, 256), 1)
     h_ref[...] = parity_signs(r, c).astype(jnp.bfloat16)
@@ -108,6 +126,23 @@
 
         lax.fori_loop(0, 8 // UNROLL, body, 0)
 
+    def targets_to(j):
+        return pltpu.make_async_remote_copy(
+            src_ref=tgt.at[me],
+            dst_ref=tgt.at[me],
+            send_sem=send_sems.at[j],
+            recv_sem=recv_sems.at[j],
+            device_id={"dp": lax.rem(me + j, 32)},
+            device_id_type=MESH,
+        )
+
+    def send_targets(j, carry):
+        targets_to(j).start()
+        return carry
+
+    pl.semaphore_wait(barrier, 34)
+    own_targets.wait()
+    lax.fori_loop(1, 32, send_targets, 0)
     fetch(0, xa, 0).wait()
     stage(0, xa, sa, None)
     fetch(2, xa, 0).start()
@@ -174,74 +209,31 @@
         return carry
 
     lax.fori_loop(0, 8, pick, 0)
-    o_ref[...] = code[...].astype(jnp.bfloat16)
-
-
-def local_terms(gradients, sign_seed, sample_index):
-    x = gradients.reshape(2, 32768, 128).transpose(1, 0, 2).reshape(512, 128, 128)
-    vmem = pltpu.VMEM
-    return pl.pallas_call(
-        local_kernel,
-        out_shape=jax.ShapeDtypeStruct((4, 2, 16, 128), jnp.bfloat16),
-        in_specs=[
-            pl.BlockSpec(memory_space=pltpu.SMEM),
-            pl.BlockSpec(memory_space=pltpu.VMEM),
-            pl.BlockSpec(memory_space=pl.ANY),
-        ],
-        out_specs=pl.BlockSpec(memory_space=pltpu.VMEM),
-        scratch_shapes=[
-            vmem((32, 128, 128), jnp.bfloat16),
-            vmem((32, 128, 128), jnp.bfloat16),
-            vmem((16, 128, 256), jnp.bfloat16),
-            vmem((16, 128, 256), jnp.bfloat16),
-            vmem((16, 16, 256, 128), jnp.bfloat16),
-            vmem((16, 4096, 128), jnp.float32),
-            vmem((1024, 128), jnp.float32),
-            vmem((256, 256), jnp.bfloat16),
-            vmem((128, 128), jnp.bfloat16),
-            vmem((4, 2, 16, 128), jnp.float32),
-            vmem((64, 128), jnp.int32),
-            pltpu.SMEM((64, 128), jnp.int32),
-            pltpu.SemaphoreType.DMA((2,)),
-            pltpu.SemaphoreType.DMA,
-        ],
-        compiler_params=pltpu.CompilerParams(vmem_limit_bytes=61 * 1024 * 1024),
-        cost_estimate=pl.CostEstimate(flops=9_000_000_000, bytes_accessed=17_000_000, transcendentals=0),
-    )(sign_seed, sample_index.reshape(64, 128), x)
-
-
-NT_DIMS = (((1,), (1,)), ((), ()))
-
-
-def score_kernel(term_ref, group_ref, target_hbm, scores_ref, means_ref, tgt, got, lhs, part, sems, tsem):
-    feat = lax.axis_index("feat")
-    target_copy = pltpu.make_async_copy(target_hbm, tgt, tsem)
-    target_copy.start()
-    barrier = pltpu.get_barrier_semaphore()
-    peers = [lax.rem(feat + d, 4) for d in (1, 2, 3)]
-    for peer in peers:
-        pl.semaphore_signal(barrier, inc=1, device_id={"feat": peer}, device_id_type=pl.DeviceIdType.MESH)
-    pl.semaphore_wait(barrier, 3)
+    term[...] = code[...].astype(jnp.bfloat16)
 
     def to_peer(source, landing, slot, d):
         return pltpu.make_async_remote_copy(
             src_ref=source,
             dst_ref=landing,
-            send_sem=sems.at[slot, 0, d],
-            recv_sem=sems.at[slot, 1, d],
+            send_sem=feat_sems.at[slot, 0, d],
+            recv_sem=feat_sems.at[slot, 1, d],
             device_id={"feat": peers[d]},
-            device_id_type=pl.DeviceIdType.MESH,
+            device_id_type=MESH,
         )
 
-    terms = [to_peer(term_ref.at[peers[d]], got.at[d], 0, d) for d in range(3)]
+    terms = [to_peer(term.at[peers[d]], got.at[d], 0, d) for d in range(3)]
     for copy in terms:
         copy.start()
-    target_copy.wait()
+    def wait_targets(j, carry):
+        targets_to(j).wait()
+        return carry
+
+    lax.fori_loop(1, 32, wait_targets, 0)
     squares = []
     for b in range(4):
         total = jnp.zeros((128, 128), jnp.float32)
         for r in range(16):
-            wide = tgt[b * 128 : (b + 1) * 128, r * 128 : (r + 1) * 128].astype(jnp.float32)
+            wide = tgt[b * 8 : (b + 1) * 8, :, r * 128 : (r + 1) * 128].reshape(128, 128).astype(jnp.float32)
             total = total + wide * wide
         squares.append(total)
     squares = jnp.concatenate(squares, axis=0)
@@ -251,7 +243,7 @@
     )
     for copy in terms:
         copy.wait()
-    own = term_ref[feat].astype(jnp.float32)
+    own = term[feat].astype(jnp.float32)
     for d in range(3):
         own = own + got[d].astype(jnp.float32)
     sketch = own.astype(jnp.bfloat16).astype(jnp.float32)
@@ -262,7 +254,7 @@
     wide = lhs[...]
     own_squares = jnp.sum(wide * wide, axis=1, keepdims=True)
     dots = lax.dot_general(
-        wide.astype(jnp.bfloat16), tgt[...], NT_DIMS, preferred_element_type=jnp.float32
+        wide.astype(jnp.bfloat16), tgt[...].reshape(512, 2048), NT_DIMS, preferred_element_type=jnp.float32
     )
     part[feat, 0] = dots
     part[feat, 1] = target_squares
@@ -288,35 +280,52 @@
 
 
 def shards(gradients, sign_seed, sample_index, target_sketches, target_group):
-    feat = lax.axis_index("feat")
-    share = lax.dynamic_slice(target_sketches, (0, feat * 2048), (16, 2048))
-    targets = lax.all_gather(share, "dp", axis=0, tiled=True)
-    terms = local_terms(gradients, sign_seed, sample_index)
+    x = gradients.reshape(2, 32768, 128).transpose(1, 0, 2).reshape(512, 128, 128)
     vmem = pltpu.VMEM
+    whole = pl.BlockSpec(memory_space=pltpu.VMEM)
     return pl.pallas_call(
-        score_kernel,
+        whole_kernel,
         out_shape=(
             jax.ShapeDtypeStruct((2, 512), jnp.float32),
             jax.ShapeDtypeStruct((2, TASKS), jnp.float32),
         ),
         in_specs=[
-            pl.BlockSpec(memory_space=pltpu.VMEM),
-            pl.BlockSpec(memory_space=pltpu.VMEM),
+            pl.BlockSpec(memory_space=pltpu.SMEM),
+            whole,
+            whole,
+            pl.BlockSpec(memory_space=pl.ANY),
             pl.BlockSpec(memory_space=pl.ANY),
         ],
-        out_specs=(pl.BlockSpec(memory_space=pltpu.VMEM), pl.BlockSpec(memory_space=pltpu.VMEM)),
+        out_specs=(whole, whole),
         scratch_shapes=[
-            vmem((512, 2048), jnp.bfloat16),
+            vmem((32, 128, 128), jnp.bfloat16),
+            vmem((32, 128, 128), jnp.bfloat16),
+            vmem((16, 128, 256), jnp.bfloat16),
+            vmem((16, 128, 256), jnp.bfloat16),
+            vmem((16, 16, 256, 128), jnp.bfloat16),
+            vmem((16, 4096, 128), jnp.float32),
+            vmem((1024, 128), jnp.float32),
+            vmem((256, 256), jnp.bfloat16),
+            vmem((128, 128), jnp.bfloat16),
+            vmem((4, 2, 16, 128), jnp.float32),
+            vmem((64, 128), jnp.int32),
+            pltpu.SMEM((64, 128), jnp.int32),
+            vmem((4, 2, 16, 128), jnp.bfloat16),
             vmem((3, 2, 16, 128), jnp.bfloat16),
             vmem((8, 2048), jnp.float32),
+            vmem((32, 16, 2048), jnp.bfloat16),
             vmem((4, 3, 8, 512), jnp.float32),
+            pltpu.SemaphoreType.DMA((2,)),
+            pltpu.SemaphoreType.DMA,
+            pltpu.SemaphoreType.DMA,
+            pltpu.SemaphoreType.DMA((32,)),
+            pltpu.SemaphoreType.DMA((32,)),
             pltpu.SemaphoreType.DMA((2, 2, 3)),
-            pltpu.SemaphoreType.DMA,
         ],
         compiler_params=pltpu.CompilerParams(
-            collective_id=0, has_side_effects=True, vmem_limit_bytes=32 * 1024 * 1024
+            collective_id=0, has_side_effects=True, vmem_limit_bytes=62 * 1024 * 1024
         ),
-    )(terms, target_group.reshape(1, 512), targets)
+    )(sign_seed, sample_index.reshape(64, 128), target_group.reshape(1, 512), target_sketches, x)
 
 
 def solution(mesh):

time: 80.3 us -> 56.6 us (0.70)
  between operations: 14.1 us -> 0.64 us
  waiting for transfers between devices: 12.8 us -> 0 us
  Pallas kernels: 46.9 us -> 52.4 us
  local copies, waits for them, and re-layouts: 5.02 us -> 2.48 us
    all_gather x1 -> x0, waiting for transfers between devices: 12.8 us -> none  [shards(): targets = lax.all_gather(share, 'dp', axis=0, tiled=True)]
    pallas_call x2 -> x1, Pallas kernels: 46.9 us -> 52.4 us  [shards(): pl.pallas_call(whole_kernel, out_shape=(jax.ShapeDtypeStruct((2, 512), jn...]
    unnamed x10 -> x2, local copies, waits for them, and re-layouts: 4.4 us -> 2.48 us
  transfers between devices with their start and end apart: 1 -> 0, of which waited for: 1 -> 0; matrix products, arithmetic and copies ran while one was open for 0% -> 0% of each run, Pallas kernels for 46% -> 0%
where the time goes in v2:
time: 56.6 us; the launch traced here: 55.5 us
  Pallas kernels  52.4 us (93%)
  local copies, waits for them, and re-layouts  2.48 us (4%)
  between operations  0.64 us (1%)
    pallas_call x1, Pallas kernels, shards(): pl.pallas_call(whole_kernel, out_shape=(jax.ShapeDtypeStruct((2, 512), jn...  52.4 us
    unnamed x2, local copies, waits for them, and re-layouts  2.48 us

profile of v2, /device:TPU:1, one launch (start us, length us, event | category | flops | bytes accessed | tf_op | source)
XLA Modules:
  0.0 55.5 jit_solution(3673881517526230048)
XLA Ops:
  0.6 52.4 %shard_map.68 = (f32[2,512]{1,0:T(2,128)}, f32[2,16]{1,0:T(2,128)}) custom-call(s32[3]{0:T(128)} %seed_ref.1, s32[64,128]{1,0:T(8,128)} %bitcast.8, s32[1,512]{1,0:T(1,128)} %bitcast.9, bf16[16,8192]{1,0:T(8,128)(2,1)} %target_hbm.1, bf16[512,128,128]{2,1,0:T(8,128)(2,1)} %bitcast.7), custom_call_target="tpu_custom_call" | custom-call | tf_op jit(solution)/shard_map/pallas_call | solution.py:286
  53.1 1.3 %copy.10 = f32[2,512]{1,0:T(2,128)} copy(f32[2,512]{1,0:T(2,128)} %get-tuple-element.4) | data formatting | bytes 8192
  54.3 1.2 %copy.11 = f32[2,16]{1,0:T(2,128)} copy(f32[2,16]{1,0:T(2,128)} %get-tuple-element.5) | data formatting | bytes 256

commit v3 on v2

--- a/solution.py
+++ b/solution.py
@@ -46,23 +46,30 @@
     return pl.multiple_of(value, by)
 
 
-def whole_kernel(seed_ref, lane_ref, group_ref, target_hbm, x_hbm, scores_ref, means_ref, xa, xb, sa, sb, y, t, g,
-                 h_ref, w_ref, code, idx_v, idx_s, term, got, lhs, tgt, part,
-                 sems, isem, tsem, send_sems, recv_sems, feat_sems):
+def whole_kernel(
+    seed_hbm, lane_hbm, group_hbm, target_hbm, x_hbm,
+    scores_ref, means_ref,
+    xbuf, sa, sb, y, t, g, h_ref, w_ref, code, seed_ref, lane_ref, group_ref, idx_v, idx_a, idx_b,
+    term, got, lhs, tgt, part,
+    x_sems, in_sems, idx_sems, send_sems, recv_sems, feat_sems,
+):
     feat = lax.axis_index("feat")
     me = lax.axis_index("dp")
-    low = lane_ref[...] & 4194303
-    idx_v[...] = ((low >> 13) << 7) | (low & 127)
-    index_copy = pltpu.make_async_copy(idx_v, idx_s, isem)
-    index_copy.start()
-
-    def fetch(n, buf, which):
-        return pltpu.make_async_copy(x_hbm.at[pl.ds(n * 32, 32), :, :], buf, sems.at[which])
-
-    fetch(0, xa, 0).start()
-    fetch(1, xb, 1).start()
+
+    def fetch(n):
+        slot = n & 3
+        return pltpu.make_async_copy(x_hbm.at[pl.ds(n * 32, 32), :, :], xbuf.at[slot], x_sems.at[slot])
+
+    seed_copy = pltpu.make_async_copy(seed_hbm, seed_ref, in_sems.at[0])
+    lane_copy = pltpu.make_async_copy(lane_hbm, lane_ref, in_sems.at[1])
+    group_copy = pltpu.make_async_copy(group_hbm, group_ref, in_sems.at[2])
     share = target_hbm.at[:, pl.ds(aligned(feat * 2048, 2048), 2048)]
-    own_targets = pltpu.make_async_copy(share, tgt.at[me], tsem)
+    own_targets = pltpu.make_async_copy(share, tgt.at[me], in_sems.at[3])
+    seed_copy.start()
+    for n in range(4):
+        fetch(n).start()
+    lane_copy.start()
+    group_copy.start()
     own_targets.start()
     barrier = pltpu.get_barrier_semaphore()
     peers = [lax.rem(feat + d, 4) for d in (1, 2, 3)]
@@ -80,6 +87,7 @@
     r = lax.broadcasted_iota(jnp.int32, (128, 128), 0)
     c = lax.broadcasted_iota(jnp.int32, (128, 128), 1)
     w_ref[...] = jnp.where((r >> 6) == (c & 1), parity_signs(r & 63, c >> 1), 0.0).astype(jnp.bfloat16)
+    seed_copy.wait()
     s0, s1, s2 = seed_ref[0], seed_ref[1], seed_ref[2] * 2048
     rows = lax.broadcasted_iota(jnp.int32, (8, 128), 0)
     cols = lax.broadcasted_iota(jnp.int32, (8, 128), 1)
@@ -114,14 +122,14 @@
         y[n, pair * 2] = out[:, :128]
         y[n, pair * 2 + 1] = out[:, 128:]
 
-    def stage(n, x_ref, s_write, s_read):
+    def stage(n, s_write, s_read, signs=True):
         def body(i, carry):
             if s_read is not None:
                 for a in range(UNROLL):
                     transform(n - 1, i * UNROLL + a, s_read)
-            if x_ref is not None:
+            if signs:
                 for a in range(UNROLL):
-                    sign(n, i * UNROLL + a, x_ref, s_write)
+                    sign(n, i * UNROLL + a, xbuf.at[n & 3], s_write)
             return carry
 
         lax.fori_loop(0, 8 // UNROLL, body, 0)
@@ -140,31 +148,44 @@
         targets_to(j).start()
         return carry
 
+    fetch(0).wait()
+    stage(0, sa, None)
+    fetch(4).start()
     pl.semaphore_wait(barrier, 34)
     own_targets.wait()
     lax.fori_loop(1, 32, send_targets, 0)
-    fetch(0, xa, 0).wait()
-    stage(0, xa, sa, None)
-    fetch(2, xa, 0).start()
+    lane_copy.wait()
+    low = lane_ref[...] & 4194303
+    idx_v[...] = ((low >> 13) << 7) | (low & 127)
 
     def outer(j, carry):
         n = 2 * j + 1
-        fetch(n, xb, 1).wait()
-        stage(n, xb, sb, sa)
-        fetch(n + 2, xb, 1).start()
-        fetch(n + 1, xa, 0).wait()
-        stage(n + 1, xa, sa, sb)
+        fetch(n).wait()
+        stage(n, sb, sa)
 
         @pl.when(j < CHUNKS // 2 - 2)
         def _():
-            fetch(n + 3, xa, 0).start()
+            fetch(n + 4).start()
+
+        fetch(n + 1).wait()
+        stage(n + 1, sa, sb)
+
+        @pl.when(j < CHUNKS // 2 - 3)
+        def _():
+            fetch(n + 5).start()
 
         return carry
 
     lax.fori_loop(0, CHUNKS // 2 - 1, outer, 0)
-    fetch(CHUNKS - 1, xb, 1).wait()
-    stage(CHUNKS - 1, xb, sb, sa)
-    stage(CHUNKS, None, None, sb)
+    fetch(CHUNKS - 1).wait()
+    stage(CHUNKS - 1, sb, sa)
+    stage(CHUNKS, None, sb, signs=False)
+
+    def indices(kb, idx_s, which):
+        return pltpu.make_async_copy(idx_v.at[pl.ds(aligned(kb * 8, 8), 8), :], idx_s, idx_sems.at[which])
+
+    indices(0, idx_a, 0).start()
+    indices(1, idx_b, 1).start()
 
     def across(i, carry):
         m = i >> 2
@@ -177,21 +198,21 @@
 
     lax.fori_loop(0, 64, across, 0)
     flat = t.reshape(65536, 128)
-    index_copy.wait()
-
-    def pick(kb, carry):
-        def row(j, inner):
+
+    def pick(i, half, idx_s):
+        kb = 2 * i + half
+        indices(kb, idx_s, half).wait()
+        for j in range(8):
             for a in range(128):
-                at = idx_s[kb * 8 + j, a]
-                g[pl.ds(j * 128 + a, 1), :] = flat[pl.ds(at, 1), :]
-            return inner
-
-        lax.fori_loop(0, 8, row, 0)
+                at = idx_s[j, a]
+                g[j * 128 + a : j * 128 + a + 1, :] = flat[pl.ds(at, 1), :]
+
+        @pl.when(i < 3)
+        def _():
+            indices(kb + 2, idx_s, half).start()
+
         out = lax.dot_general(
-            w_ref[...],
-            g[...].astype(jnp.bfloat16),
-            (((1,), (1,)), ((), ())),
-            preferred_element_type=jnp.float32,
+            w_ref[...], g[...].astype(jnp.bfloat16), NT_DIMS, preferred_element_type=jnp.float32
         )
         place = lax.broadcasted_iota(jnp.int32, (64, 128), 0)
         for j in range(8):
@@ -200,15 +221,17 @@
             common = (picked >> 22) & feat
             scale = jnp.where((((common >> 1) ^ common) & 1) == 1, -1.0 / 4096, 1.0 / 4096)
             for e in range(2):
-                third = jnp.sum(
-                    jnp.where(hit, out[e * 64 : (e + 1) * 64, j * 128 : (j + 1) * 128], 0.0),
-                    axis=0,
-                    keepdims=True,
-                )
-                code[kb >> 1, e, pl.ds((kb & 1) * 8 + j, 1), :] = third * scale
-        return carry
-
-    lax.fori_loop(0, 8, pick, 0)
+                mine = jnp.where(hit, out[e * 64 : (e + 1) * 64, j * 128 : (j + 1) * 128], 0.0)
+                third = jnp.sum(mine, axis=0, keepdims=True)
+                row = half * 8 + j
+                code[i, e, row : row + 1, :] = third * scale
+
+    def pick_two(i, carry):
+        pick(i, 0, idx_a)
+        pick(i, 1, idx_b)
+        return carry
+
+    lax.fori_loop(0, 4, pick_two, 0)
     term[...] = code[...].astype(jnp.bfloat16)
 
     def to_peer(source, landing, slot, d):
@@ -262,19 +285,23 @@
     parts = [to_peer(part.at[feat], part.at[feat], 1, d) for d in range(3)]
     for copy in parts:
         copy.start()
+    group_copy.wait()
     member = (lax.broadcasted_iota(jnp.int32, (128, 512), 0) == group_ref[...]).astype(jnp.float32)
+    member = member.astype(jnp.bfloat16)
     for copy in parts:
         copy.wait()
     whole = (part[0] + part[1]) + (part[2] + part[3])
     scores = whole[0] * lax.rsqrt(whole[2] + EPS) * lax.rsqrt(whole[1] + EPS) * math.sqrt(8192)
     at = lax.broadcasted_iota(jnp.int32, (8, 512), 0)
-    sums = lax.dot_general(
-        jnp.where(at < 2, scores, 1.0),
-        member,
-        NT_DIMS,
-        precision=lax.Precision.HIGHEST,
-        preferred_element_type=jnp.float32,
-    )
+    rest = scores
+    sums = jnp.zeros((8, 128), jnp.float32)
+    for piece in range(3):
+        top = rest.astype(jnp.bfloat16)
+        rest = rest - top.astype(jnp.float32)
+        filled = jnp.where(at < 2, top.astype(jnp.float32), 1.0 if piece == 0 else 0.0)
+        sums = sums + lax.dot_general(
+            filled.astype(jnp.bfloat16), member, NT_DIMS, preferred_element_type=jnp.float32
+        )
     scores_ref[...] = scores[:2]
     means_ref[...] = sums[:2, :TASKS] / sums[2:3, :TASKS]
 
@@ -283,23 +310,17 @@
     x = gradients.reshape(2, 32768, 128).transpose(1, 0, 2).reshape(512, 128, 128)
     vmem = pltpu.VMEM
     whole = pl.BlockSpec(memory_space=pltpu.VMEM)
+    dma = pltpu.SemaphoreType.DMA
     return pl.pallas_call(
         whole_kernel,
         out_shape=(
             jax.ShapeDtypeStruct((2, 512), jnp.float32),
             jax.ShapeDtypeStruct((2, TASKS), jnp.float32),
         ),
-        in_specs=[
-            pl.BlockSpec(memory_space=pltpu.SMEM),
-            whole,
-            whole,
-            pl.BlockSpec(memory_space=pl.ANY),
-            pl.BlockSpec(memory_space=pl.ANY),
-        ],
+        in_specs=[pl.BlockSpec(memory_space=pl.ANY)] * 5,
         out_specs=(whole, whole),
         scratch_shapes=[
-            vmem((32, 128, 128), jnp.bfloat16),
-            vmem((32, 128, 128), jnp.bfloat16),
+            vmem((4, 32, 128, 128), jnp.bfloat16),
             vmem((16, 128, 256), jnp.bfloat16),
             vmem((16, 128, 256), jnp.bfloat16),
             vmem((16, 16, 256, 128), jnp.bfloat16),
@@ -308,22 +329,26 @@
             vmem((256, 256), jnp.bfloat16),
             vmem((128, 128), jnp.bfloat16),
             vmem((4, 2, 16, 128), jnp.float32),
+            pltpu.SMEM((3,), jnp.int32),
             vmem((64, 128), jnp.int32),
-            pltpu.SMEM((64, 128), jnp.int32),
+            vmem((1, 512), jnp.int32),
+            vmem((64, 128), jnp.int32),
+            pltpu.SMEM((8, 128), jnp.int32),
+            pltpu.SMEM((8, 128), jnp.int32),
             vmem((4, 2, 16, 128), jnp.bfloat16),
             vmem((3, 2, 16, 128), jnp.bfloat16),
             vmem((8, 2048), jnp.float32),
             vmem((32, 16, 2048), jnp.bfloat16),
             vmem((4, 3, 8, 512), jnp.float32),
-            pltpu.SemaphoreType.DMA((2,)),
-            pltpu.SemaphoreType.DMA,
-            pltpu.SemaphoreType.DMA,
-            pltpu.SemaphoreType.DMA((32,)),
-            pltpu.SemaphoreType.DMA((32,)),
-            pltpu.SemaphoreType.DMA((2, 2, 3)),
+            dma((4,)),
+            dma((4,)),
+            dma((2,)),
+            dma((32,)),
+            dma((32,)),
+            dma((2, 2, 3)),
         ],
         compiler_params=pltpu.CompilerParams(
-            collective_id=0, has_side_effects=True, vmem_limit_bytes=62 * 1024 * 1024
+            collective_id=0, has_side_effects=True, vmem_limit_bytes=60 * 1024 * 1024
         ),
     )(sign_seed, sample_index.reshape(64, 128), target_group.reshape(1, 512), target_sketches, x)
 

time: 56.6 us -> 51.8 us (0.915); the launches traced: 55.5 us -> 51.5 us
  Pallas kernels: 52.4 us -> 48.3 us
    pallas_call x1, Pallas kernels: 52.4 us -> 48.3 us  [shards(): pl.pallas_call(whole_kernel, out_shape=(jax.ShapeDtypeStruct((2, 512), jn...]
where the time goes in v3:
time: 51.8 us; the launch traced here: 51.5 us
  Pallas kernels  48.3 us (93%)
  local copies, waits for them, and re-layouts  2.48 us (5%)
  between operations  0.64 us (1%)
    pallas_call x1, Pallas kernels, shards(): pl.pallas_call(whole_kernel, out_shape=(jax.ShapeDtypeStruct((2, 512), jn...  48.3 us
    unnamed x2, local copies, waits for them, and re-layouts  2.48 us

profile of v3, /device:TPU:1, one launch (start us, length us, event | category | flops | bytes accessed | tf_op | source)
XLA Modules:
  0.0 51.5 jit_solution(9317847488810343582)
XLA Ops:
  0.6 48.3 %shard_map.68 = (f32[2,512]{1,0:T(2,128)}, f32[2,16]{1,0:T(2,128)}) custom-call(s32[3]{0:T(128)} %seed_hbm.1, s32[64,128]{1,0:T(8,128)} %bitcast.8, s32[1,512]{1,0:T(1,128)} %bitcast.9, bf16[16,8192]{1,0:T(8,128)(2,1)} %target_hbm.1, bf16[512,128,128]{2,1,0:T(8,128)(2,1)} %bitcast.7), custom_call_target="tpu_custom_call" | custom-call | tf_op jit(solution)/shard_map/pallas_call | solution.py:314
  49.0 1.3 %copy.10 = f32[2,512]{1,0:T(2,128)} copy(f32[2,512]{1,0:T(2,128)} %get-tuple-element.4) | data formatting | bytes 8192
  50.2 1.2 %copy.11 = f32[2,16]{1,0:T(2,128)} copy(f32[2,16]{1,0:T(2,128)} %get-tuple-element.5) | data formatting | bytes 256

commit v4 on v3

--- a/solution.py
+++ b/solution.py
@@ -49,7 +49,7 @@
 def whole_kernel(
     seed_hbm, lane_hbm, group_hbm, target_hbm, x_hbm,
     scores_ref, means_ref,
-    xbuf, sa, sb, y, t, g, h_ref, w_ref, code, seed_ref, lane_ref, group_ref, idx_v, idx_a, idx_b,
+    xbuf, sa, sb, t, g, h_ref, w_ref, code, seed_ref, lane_ref, group_ref, idx_v, idx_a, idx_b,
     term, got, lhs, tgt, part,
     x_sems, in_sems, idx_sems, send_sems, recv_sems, feat_sems,
 ):
@@ -116,20 +116,18 @@
 
     def transform(n, pair, s_ref):
         rhs = s_ref[pl.ds(pair * 2, 2), :, :].reshape(256, 256)
-        out = lax.dot_general(
-            h_ref[...], rhs, (((1,), (1,)), ((), ())), preferred_element_type=jnp.float32
-        ).astype(jnp.bfloat16)
-        y[n, pair * 2] = out[:, :128]
-        y[n, pair * 2 + 1] = out[:, 128:]
+        out = lax.dot_general(h_ref[...], rhs, NT_DIMS, preferred_element_type=jnp.float32)
+        at = aligned(pair * 512, 512)
+        t[n, pl.ds(at, 256), :] = out[:, :128]
+        t[n, pl.ds(at + 256, 256), :] = out[:, 128:]
 
     def stage(n, s_write, s_read, signs=True):
         def body(i, carry):
-            if s_read is not None:
-                for a in range(UNROLL):
+            for a in range(UNROLL):
+                if signs:
+                    sign(n, i * UNROLL + a, xbuf.at[n & 3], s_write)
+                if s_read is not None:
                     transform(n - 1, i * UNROLL + a, s_read)
-            if signs:
-                for a in range(UNROLL):
-                    sign(n, i * UNROLL + a, xbuf.at[n & 3], s_write)
             return carry
 
         lax.fori_loop(0, 8 // UNROLL, body, 0)
@@ -188,15 +186,14 @@
     indices(1, idx_b, 1).start()
 
     def across(i, carry):
-        m = i >> 2
-        o = aligned((i & 3) * 64, 64)
-        for a in range(4):
-            vals = butterflies([y[n, m, pl.ds(o + a * 16, 16), :] for n in range(CHUNKS)])
+        for a in range(16):
+            rows8 = pl.ds(aligned(i * 128, 128) + a * 8, 8)
+            vals = butterflies([t[n, rows8, :] for n in range(CHUNKS)])
             for n in range(CHUNKS):
-                t[n, pl.ds(aligned(i * 64 + a * 16, 16), 16), :] = vals[n].astype(jnp.float32)
-        return carry
-
-    lax.fori_loop(0, 64, across, 0)
+                t[n, rows8, :] = vals[n]
+        return carry
+
+    lax.fori_loop(0, 32, across, 0)
     flat = t.reshape(65536, 128)
 
     def pick(i, half, idx_s):
@@ -317,13 +314,12 @@
             jax.ShapeDtypeStruct((2, 512), jnp.float32),
             jax.ShapeDtypeStruct((2, TASKS), jnp.float32),
         ),
-        in_specs=[pl.BlockSpec(memory_space=pl.ANY)] * 5,
+        in_specs=[pl.BlockSpec(memory_space=pltpu.HBM)] * 5,
         out_specs=(whole, whole),
         scratch_shapes=[
             vmem((4, 32, 128, 128), jnp.bfloat16),
             vmem((16, 128, 256), jnp.bfloat16),
             vmem((16, 128, 256), jnp.bfloat16),
-            vmem((16, 16, 256, 128), jnp.bfloat16),
             vmem((16, 4096, 128), jnp.float32),
             vmem((1024, 128), jnp.float32),
             vmem((256, 256), jnp.bfloat16),
@@ -348,7 +344,7 @@
             dma((2, 2, 3)),
         ],
         compiler_params=pltpu.CompilerParams(
-            collective_id=0, has_side_effects=True, vmem_limit_bytes=60 * 1024 * 1024
+            collective_id=0, has_side_effects=True, vmem_limit_bytes=48 * 1024 * 1024
         ),
     )(sign_seed, sample_index.reshape(64, 128), target_group.reshape(1, 512), target_sketches, x)
 

time: 51.8 us -> 53.6 us (1.035)
  local copies, waits for them, and re-layouts: 2.48 us -> 4.19 us
    unnamed x2 -> x10, local copies, waits for them, and re-layouts: 2.48 us -> 4.19 us
where the time goes in v4:
time: 53.6 us; the launch traced here: 53.4 us
  Pallas kernels  48.6 us (91%)
  local copies, waits for them, and re-layouts  4.19 us (8%)
  between operations  0.65 us (1%)
    pallas_call x1, Pallas kernels, shards(): pl.pallas_call(whole_kernel, out_shape=(jax.ShapeDtypeStruct((2, 512), jn...  48.6 us
    unnamed x10, local copies, waits for them, and re-layouts  4.19 us

profile of v4, /device:TPU:1, one launch (start us, length us, event | category | flops | bytes accessed | tf_op | source)
XLA Modules:
  0.0 53.4 jit_solution(7861045974291803790)
XLA Ops:
  0.6 0.0 copy-start
  0.6 0.9 %copy-done = bf16[16,8192]{1,0:T(8,128)(2,1)S(1)} copy-done((bf16[16,8192]{1,0:T(8,128)(2,1)S(1)}, bf16[16,8192]{1,0:T(8,128)(2,1)}, u32[]{:S(2)}) %copy-start) | copy-done | bytes 262168
  1.6 0.0 copy-start.1
  1.6 0.8 %copy-done.1 = s32[8192]{0:T(1024)S(1)} copy-done((s32[8192]{0:T(1024)S(1)}, s32[8192]{0:T(1024)}, u32[]{:S(2)}) %copy-start.1) | copy-done | bytes 32792
  2.3 0.0 copy-start.2
  2.3 0.7 %copy-done.2 = s32[512]{0:T(512)S(1)} copy-done((s32[512]{0:T(512)S(1)}, s32[512]{0:T(512)}, u32[]{:S(2)}) %copy-start.2) | copy-done | bytes 2072
  3.0 0.0 copy-start.3
  3.0 0.7 %copy-done.3 = s32[3]{0:T(128)S(1)} copy-done((s32[3]{0:T(128)S(1)}, s32[3]{0:T(128)}, u32[]{:S(2)}) %copy-start.3) | copy-done | bytes 36
  3.7 48.6 %shard_map.68 = (f32[2,512]{1,0:T(2,128)S(1)}, f32[2,16]{1,0:T(2,128)S(1)}) custom-call(s32[3]{0:T(128)S(1)} %copy-done.3, s32[64,128]{1,0:T(8,128)S(1)} %bitcast.7, s32[1,512]{1,0:T(1,128)S(1)} %bitcast.8, bf16[16,8192]{1,0:T(8,128)(2,1)S(1)} %copy-done, bf16[512,128,128]{2,1,0:T(8,128)(2,1)} %bitcast.9), custom_call_target="tpu_custom_call" | custom-call | tf_op jit(solution)/shard_map/pallas_call | solution.py:311
  52.2 0.6 %copy.10 = f32[2,512]{1,0:T(2,128)} copy(f32[2,512]{1,0:T(2,128)S(1)} %get-tuple-element.4) | data formatting | bytes 8192
  52.8 0.6 %copy.11 = f32[2,16]{1,0:T(2,128)} copy(f32[2,16]{1,0:T(2,128)S(1)} %get-tuple-element.5) | data formatting | bytes 256
Async XLA Ops:
  0.6 1.0 %copy-start = (bf16[16,8192]{1,0:T(8,128)(2,1)S(1)}, bf16[16,8192]{1,0:T(8,128)(2,1)}, u32[]{:S(2)}) copy-start(bf16[16,8192]{1,0:T(8,128)(2,1)} %target_hbm.1) | copy-start | bytes 786436
  1.6 0.8 %copy-start.1 = (s32[8192]{0:T(1024)S(1)}, s32[8192]{0:T(1024)}, u32[]{:S(2)}) copy-start(s32[8192]{0:T(1024)} %param.7) | copy-start | bytes 98308
  2.3 0.7 %copy-start.2 = (s32[512]{0:T(512)S(1)}, s32[512]{0:T(512)}, u32[]{:S(2)}) copy-start(s32[512]{0:T(512)} %param.9) | copy-start | bytes 6148
  3.0 0.7 %copy-start.3 = (s32[3]{0:T(128)S(1)}, s32[3]{0:T(128)}, u32[]{:S(2)}) copy-start(s32[3]{0:T(128)} %seed_hbm.1) | copy-start | bytes 40

commit v5 on v4

--- a/solution.py
+++ b/solution.py
@@ -49,7 +49,7 @@
 def whole_kernel(
     seed_hbm, lane_hbm, group_hbm, target_hbm, x_hbm,
     scores_ref, means_ref,
-    xbuf, sa, sb, t, g, h_ref, w_ref, code, seed_ref, lane_ref, group_ref, idx_v, idx_a, idx_b,
+    xbuf, sa, sb, t, ga, gb, h_ref, w_ref, code, seed_ref, lane_ref, group_ref, idx_v, idx_a, idx_b,
     term, got, lhs, tgt, part,
     x_sems, in_sems, idx_sems, send_sems, recv_sems, feat_sems,
 ):
@@ -66,7 +66,7 @@
     share = target_hbm.at[:, pl.ds(aligned(feat * 2048, 2048), 2048)]
     own_targets = pltpu.make_async_copy(share, tgt.at[me], in_sems.at[3])
     seed_copy.start()
-    for n in range(4):
+    for n in range(2):
         fetch(n).start()
     lane_copy.start()
     group_copy.start()
@@ -147,6 +147,8 @@
         return carry
 
     fetch(0).wait()
+    for n in (2, 3):
+        fetch(n).start()
     stage(0, sa, None)
     fetch(4).start()
     pl.semaphore_wait(barrier, 34)
@@ -196,39 +198,50 @@
     lax.fori_loop(0, 32, across, 0)
     flat = t.reshape(65536, 128)
 
-    def pick(i, half, idx_s):
-        kb = 2 * i + half
-        indices(kb, idx_s, half).wait()
-        for j in range(8):
-            for a in range(128):
-                at = idx_s[j, a]
-                g[j * 128 + a : j * 128 + a + 1, :] = flat[pl.ds(at, 1), :]
-
-        @pl.when(i < 3)
-        def _():
-            indices(kb + 2, idx_s, half).start()
-
+    place = lax.broadcasted_iota(jnp.int32, (64, 128), 0)
+
+    def finish(rows, quarter, at):
         out = lax.dot_general(
-            w_ref[...], g[...].astype(jnp.bfloat16), NT_DIMS, preferred_element_type=jnp.float32
+            w_ref[...], rows.astype(jnp.bfloat16), NT_DIMS, preferred_element_type=jnp.float32
         )
-        place = lax.broadcasted_iota(jnp.int32, (64, 128), 0)
-        for j in range(8):
-            picked = lane_ref[pl.ds(kb * 8 + j, 1), :]
+        for j in range(2):
+            picked = lane_ref[pl.ds(quarter * 16 + at + j, 1), :]
             hit = place == ((picked >> 7) & 63)
             common = (picked >> 22) & feat
             scale = jnp.where((((common >> 1) ^ common) & 1) == 1, -1.0 / 4096, 1.0 / 4096)
             for e in range(2):
                 mine = jnp.where(hit, out[e * 64 : (e + 1) * 64, j * 128 : (j + 1) * 128], 0.0)
                 third = jnp.sum(mine, axis=0, keepdims=True)
-                row = half * 8 + j
-                code[i, e, row : row + 1, :] = third * scale
+                code[quarter, e, at + j : at + j + 1, :] = third * scale
+
+    def pick(kb, which, g, before, quarter, at):
+        idx_s = (idx_a, idx_b)[which]
+        indices(kb, idx_s, which).wait()
+        for j in range(8):
+            if before is not None and j % 2 == 0:
+                finish(before[j * 128 : (j + 2) * 128, :], quarter, at + j)
+            for a in range(128):
+                g[j * 128 + a : j * 128 + a + 1, :] = flat[pl.ds(idx_s[j, a], 1), :]
+
+    pick(0, 0, ga, None, 0, 0)
+    indices(2, idx_a, 0).start()
 
     def pick_two(i, carry):
-        pick(i, 0, idx_a)
-        pick(i, 1, idx_b)
-        return carry
-
-    lax.fori_loop(0, 4, pick_two, 0)
+        kb = 2 * i + 1
+        pick(kb, 1, gb, ga, i, 0)
+        indices(kb + 2, idx_b, 1).start()
+        pick(kb + 1, 0, ga, gb, i, 8)
+
+        @pl.when(i < 2)
+        def _():
+            indices(kb + 3, idx_a, 0).start()
+
+        return carry
+
+    lax.fori_loop(0, 3, pick_two, 0)
+    pick(7, 1, gb, ga, 3, 0)
+    for j in range(0, 8, 2):
+        finish(gb[j * 128 : (j + 2) * 128, :], 3, 8 + j)
     term[...] = code[...].astype(jnp.bfloat16)
 
     def to_peer(source, landing, slot, d):
@@ -322,6 +335,7 @@
             vmem((16, 128, 256), jnp.bfloat16),
             vmem((16, 4096, 128), jnp.float32),
             vmem((1024, 128), jnp.float32),
+            vmem((1024, 128), jnp.float32),
             vmem((256, 256), jnp.bfloat16),
             vmem((128, 128), jnp.bfloat16),
             vmem((4, 2, 16, 128), jnp.float32),
@@ -344,7 +358,7 @@
             dma((2, 2, 3)),
         ],
         compiler_params=pltpu.CompilerParams(
-            collective_id=0, has_side_effects=True, vmem_limit_bytes=48 * 1024 * 1024
+            collective_id=0, has_side_effects=True, vmem_limit_bytes=58 * 1024 * 1024
         ),
     )(sign_seed, sample_index.reshape(64, 128), target_group.reshape(1, 512), target_sketches, x)
 

time: 53.6 us -> 52.4 us (0.978)
  local copies, waits for them, and re-layouts: 4.19 us -> 2.48 us
    unnamed x10 -> x2, local copies, waits for them, and re-layouts: 4.19 us -> 2.48 us
    pallas_call x1, Pallas kernels: 48.6 us -> 49.1 us  [shards(): pl.pallas_call(whole_kernel, out_shape=(jax.ShapeDtypeStruct((2, 512), jn...]
where the time goes in v5:
time: 52.4 us; the launch traced here: 52.2 us
  Pallas kernels  49.1 us (94%)
  local copies, waits for them, and re-layouts  2.48 us (5%)
  between operations  0.64 us (1%)
    pallas_call x1, Pallas kernels, shards(): pl.pallas_call(whole_kernel, out_shape=(jax.ShapeDtypeStruct((2, 512), jn...  49.1 us
    unnamed x2, local copies, waits for them, and re-layouts  2.48 us

profile of v5, /device:TPU:1, one launch (start us, length us, event | category | flops | bytes accessed | tf_op | source)
XLA Modules:
  0.0 52.2 jit_solution(6301162153136915916)
XLA Ops:
  0.6 49.1 %shard_map.68 = (f32[2,512]{1,0:T(2,128)}, f32[2,16]{1,0:T(2,128)}) custom-call(s32[3]{0:T(128)} %seed_hbm.1, s32[64,128]{1,0:T(8,128)} %bitcast.8, s32[1,512]{1,0:T(1,128)} %bitcast.9, bf16[16,8192]{1,0:T(8,128)(2,1)} %target_hbm.1, bf16[512,128,128]{2,1,0:T(8,128)(2,1)} %bitcast.7), custom_call_target="tpu_custom_call" | custom-call | tf_op jit(solution)/shard_map/pallas_call | solution.py:324
  49.8 1.3 %copy.10 = f32[2,512]{1,0:T(2,128)} copy(f32[2,512]{1,0:T(2,128)} %get-tuple-element.4) | data formatting | bytes 8192
  51.0 1.2 %copy.11 = f32[2,16]{1,0:T(2,128)} copy(f32[2,16]{1,0:T(2,128)} %get-tuple-element.5) | data formatting | bytes 256
